TPU v7x, 32 devices: a whole 2x2x4 slice. The times are simulated.
32 devices in a mesh: ctx: 8 (over z, core), tp: 4 (over y, x).
Axes of the slice: x: 2, y: 2, z: 4, core: 2. Of those that a mesh axis runs over, the one named last changes fastest.
Arguments:
- queries: bfloat16 [3072, 16, 128], P('ctx', 'tp'), may hold values from -6 to 6
- key_tensor: bfloat16 [3072, 2, 128], P('ctx'), may hold values from -6 to 6
- value_tensor: bfloat16 [3072, 2, 128], P('ctx'), may hold values from -6 to 6
- attn_output: bfloat16 [3072, 16, 128], P('ctx', 'tp'), may hold values from -4 to 4
- logsumexp_rows: float32 [16, 3072], P('tp', 'ctx'), may hold values from 4 to 7
- grad_output: bfloat16 [3072, 8192], P(('ctx', 'tp')), may hold values from -6 to 6
- out_proj: bfloat16 [2048, 8192], P('tp'), may hold values from -0.0625 to 0.0625
- block_doc: int32 [24], replicated, may hold values from 0 to 5, never falling along the last dimension, each value on 1 to 12 neighbouring positions
Outputs:
- grad_query: bfloat16 [3072, 16, 128], P('ctx', 'tp')
- grad_key: bfloat16 [3072, 2, 128], P(('ctx', 'tp'))
- grad_value: bfloat16 [3072, 2, 128], P(('ctx', 'tp'))
Inputs may be any that keep to these rules, and one draw needn't show every extreme that they name: `block_doc`: document ids never fall along the sequence; one document spans 1 to 12 blocks, and some document spans exactly 12 in every draw.
All inputs are finite; a program needn't handle non-finite values.
Results may differ from a plain program's by a relative error of at most 0.012.
Values may be sent and summed in bfloat16 or wider, within the bound.
No kernel may reach another device: no remote copies, remote signals or barrier semaphores. Data moves between devices by JAX's collectives and lax.ppermute only.
A program may use at most 64 MiB of HBM per device.

v0:
```python
import jax
import jax.numpy as jnp
from jax import lax
from jax.sharding import PartitionSpec as P

QUERY_HEADS = 16
KEY_VALUE_HEADS = 2
DOCBLK = 128
RANKS_BACK = 4


def passed_along(shard, axis, by):
    peers = lax.axis_size(axis)
    pairs = [(i, i + by) for i in range(peers) if 0 <= i + by < peers]
    return lax.ppermute(shard, axis, pairs)


def from_behind(block, axis, distance):
    devices = range(lax.axis_size(axis))
    route = [((i - distance) % len(devices), i) for i in devices]
    return lax.ppermute(block, axis, route)


def doc_labels(block_doc, source_rank, row_count, block_size):
    block_count = row_count // block_size
    labels = lax.dynamic_slice_in_dim(block_doc, source_rank * block_count, block_count)
    return jnp.repeat(labels, block_size, total_repeat_length=row_count)


def tile_terms(
    allowed,
    query_block,
    gradient_block,
    logsumexp_block,
    delta_block,
    key_blk,
    value_blk,
    score_scale,
):
    scores = (
        jnp.einsum("ihd,jd->hij", query_block, key_blk, preferred_element_type=jnp.float32)
        * score_scale
    )
    prob_full = jnp.exp(jnp.where(allowed[None], scores - logsumexp_block[:, :, None], -1e30))
    dprobs = jnp.einsum(
        "ihd,jd->hij", gradient_block, value_blk, preferred_element_type=jnp.float32
    )
    dscores = (prob_full * (dprobs - delta_block[:, :, None]) * score_scale).astype(jnp.bfloat16)
    grad_q_part = jnp.einsum("hij,jd->ihd", dscores, key_blk, preferred_element_type=jnp.float32)
    grad_k_part = jnp.einsum(
        "hij,ihd->jd", dscores, query_block, preferred_element_type=jnp.float32
    )
    grad_v_part = jnp.einsum(
        "hij,ihd->jd",
        prob_full.astype(jnp.bfloat16),
        gradient_block,
        preferred_element_type=jnp.float32,
    )
    return (grad_q_part, grad_k_part, grad_v_part)


def per_device(
    queries, key_tensor, value_tensor, attn_output, logsumexp_rows, grad_output, out_proj, block_doc
):
    row_count = queries.shape[0]
    window_heads = queries.shape[1]
    head_dim = queries.shape[2]
    kv_heads = key_tensor.shape[1]
    cycle_size = lax.axis_size("ctx")
    span_ranks = min(RANKS_BACK, cycle_size // 2)
    score_scale = head_dim ** (-0.5)
    my_rank = lax.axis_index("ctx")
    group_number_index = lax.axis_index("tp") * window_heads // (QUERY_HEADS // KEY_VALUE_HEADS)
    offsets = jnp.arange(row_count, dtype=jnp.int32)
    product = lax.dot_general(
        lax.all_gather(grad_output, "tp", axis=0, tiled=True),
        out_proj,
        (((1,), (1,)), ((), ())),
        preferred_element_type=jnp.float32,
    )
    head_gradients = product.astype(jnp.bfloat16)
    head_gradients = head_gradients.reshape(row_count, window_heads, head_dim)
    delta_terms = jnp.sum(
        head_gradients.astype(jnp.float32) * attn_output.astype(jnp.float32), axis=2
    ).T
    key_mine = lax.dynamic_index_in_dim(key_tensor, group_number_index, 1, keepdims=False)
    value_mine = lax.dynamic_index_in_dim(value_tensor, group_number_index, 1, keepdims=False)

    def pair_terms(
        query_block,
        gradient_block,
        logsumexp_block,
        delta_block,
        query_rank,
        key_blk,
        value_blk,
        key_rank,
    ):
        query_pos = query_rank * row_count + offsets
        key_pos = key_rank * row_count + offsets
        query_doc = doc_labels(block_doc, query_rank, row_count, DOCBLK)
        key_doc = doc_labels(block_doc, key_rank, row_count, DOCBLK)
        allowed = (query_doc[:, None] == key_doc[None, :]) & (
            key_pos[None, :] <= query_pos[:, None]
        )
        return tile_terms(
            allowed,
            query_block,
            gradient_block,
            logsumexp_block,
            delta_block,
            key_blk,
            value_blk,
            score_scale,
        )

    first_q, first_k, first_v = pair_terms(
        queries, head_gradients, logsumexp_rows, delta_terms, my_rank, key_mine, value_mine, my_rank
    )

    def key_turn(cycle_step, carry):
        key_move, value_move, key_acc, value_acc, query_acc = carry
        key_move, value_move = passed_along((key_move, value_move), "ctx", 1)
        key_acc, value_acc = from_behind((key_acc, value_acc), "ctx", 1)
        source_rank = (my_rank - cycle_step) % cycle_size
        part_q, part_k, part_v = pair_terms(
            queries,
            head_gradients,
            logsumexp_rows,
            delta_terms,
            my_rank,
            key_move,
            value_move,
            source_rank,
        )
        return (key_move, value_move, key_acc + part_k, value_acc + part_v, query_acc + part_q)

    start_state = (key_mine, value_mine, first_k, first_v, first_q)
    final_state = lax.fori_loop(1, span_ranks + 1, key_turn, start_state)
    key_total, value_total = (
        from_behind(final_state[2].astype(jnp.bfloat16), "ctx", -span_ranks).astype(jnp.float32),
        from_behind(final_state[3].astype(jnp.bfloat16), "ctx", -span_ranks).astype(jnp.float32),
    )
    query_total = final_state[4]
    head_mask = (jnp.arange(kv_heads, dtype=jnp.int32) == group_number_index).astype(jnp.float32)
    key_full = key_total[:, None, :] * head_mask[None, :, None]
    value_full = value_total[:, None, :] * head_mask[None, :, None]
    key_part, value_part = (
        lax.psum_scatter(
            key_full.astype(jnp.bfloat16), "tp", scatter_dimension=0, tiled=True
        ).astype(jnp.float32),
        lax.psum_scatter(
            value_full.astype(jnp.bfloat16), "tp", scatter_dimension=0, tiled=True
        ).astype(jnp.float32),
    )
    return (
        query_total.astype(jnp.bfloat16),
        key_part.astype(jnp.bfloat16),
        value_part.astype(jnp.bfloat16),
    )


def solution(mesh):
    placed = (
        P("ctx", "tp", None),
        P("ctx", None, None),
        P("ctx", None, None),
        P("ctx", "tp", None),
        P("tp", "ctx"),
        P(("ctx", "tp"), None),
        P("tp", None),
        P(),
    )
    return jax.shard_map(
        per_device,
        mesh=mesh,
        in_specs=placed,
        out_specs=(
            P("ctx", "tp", None),
            P(("ctx", "tp"), None, None),
            P(("ctx", "tp"), None, None),
        ),
        check_vma=False,
    )
```

profile of v0, /device:TPU:0, one launch (start us, length us, event | category | flops | bytes accessed | tf_op | source)
XLA Modules:
  0.0 231.2 jit_solution(17869435017987135812)
XLA Ops:
  7.2 0.7 all-gather.2.cloned.1.call-update
  8.0 1.4 constant_dynamic-slice_fusion.2
  9.4 0.7 copy.80
  10.1 0.7 copy.81
  10.9 0.7 fusion.52
  11.5 1.9 select_select_fusion.2
  13.5 0.8 compare_and_fusion.2
  14.8 68.0 %all-gather.2.cloned.1.call-done = bf16[384,8192]{1,0:T(8,128)(2,1)} async-done(((bf16[96,8192]{1,0:T(8,128)(2,1)}), bf16[384,8192]{1,0:T(8,128)(2,1)}) %all-gather.2.cloned.1.call-update) | async-done | bytes 6291472 | tf_op jit(solution)/shard_map/all_gather | solution.py:76
  82.8 8.6 %convolution_convert_fusion = bf16[384,512]{1,0:T(8,128)(2,1)S(1)} fusion(bf16[384,8192]{1,0:T(8,128)(2,1)} %all-gather.2.cloned.1.call-done, bf16[512,8192]{1,0:T(8,128)(2,1)} %param.26), kind=kOutput, calls=%fused_computation.41 | convolution fusion | flops 3221422080 | bytes 15073280 | tf_op jit(solution)/shard_map/dot_general | solution.py:75
  91.4 0.7 copy-done.1
  92.2 0.8 copy_bitcast_fusion
  93.0 1.8 reshape.343
  94.8 2.3 multiply_reduce_fusion
  97.1 1.0 copy.40
  98.1 2.5 %fusion.36 = f32[384,128]{1,0:T(8,128)} fusion(f32[384,384,4]{1,0,2:T(8,128)S(1)} %fusion.41, f32[4,384]{1,0:T(4,128)} %param.24, pred[384,384]{0,1:T(8,128)(4,1)} %compare_and_fusion.2, bf16[384,512]{1,0:T(8,128)(2,1)} %copy-done.1), kind=kOutput, calls=%fused_computation.44 | convolution fusion | flops 153354240 | bytes 3102720 | tf_op jit(solution)/shard_map/hij,ihd->jd/dot_general | solution.py:53
  100.6 1.6 fusion.29
  103.5 62.0 %while.31 = (s32[]{:T(128)}, bf16[384,128]{1,0:T(8,128)(2,1)S(1)}, bf16[384,128]{1,0:T(8,128)(2,1)S(1)}, f32[384,128]{1,0:T(8,128)S(1)}, f32[384,128]{1,0:T(8,12...) while((s32[]{:T(128)}, bf16[384,128]{1,0:T(8,128)(2,1)S(1)}, ...), condition=%wide.region_2.4_spmd.clone.clone, body=%wide.region_1.3_spmd.clone.clone.sunk | while | flops 762210816 | bytes 18070140 | solution.py:139
  103.6 1.8 collective-permute-start.1
  105.4 3.7 %collective-permute-start = (bf16[384,128]{1,0:T(8,128)(2,1)S(1)}, bf16[384,128]{1,0:T(8,128)(2,1)S(1)}, u32[]{:S(2)}, u32[]{:S(2)}) collective-permute-start(bf16[384,128]{1,0:T(8,128)(2,1)S(1)} %get-tuple-element.773), channel_id=1, source_target_pairs={{0,4},{4,8},{8,12},{12,16},{16,20},{20,24},{24,28},{1,5},{5,9},{9,... | collective-permute-start | bytes 294920 | tf_op jit(solution)/shard_map/while/body/eval_jaxpr/ppermute | solution.py:15
  109.1 1.6 collective-permute-start.2
  110.8 0.7 fusion.95
  111.5 0.7 fusion.94
  112.1 2.0 select_select_fusion.4
  114.1 2.0 iota_add_fusion.6
  116.8 0.9 fusion.96
  117.7 0.6 fusion.99
  118.3 0.7 fusion.98
  119.6 2.0 collective-permute-start.1
  121.6 3.4 %collective-permute-start = (bf16[384,128]{1,0:T(8,128)(2,1)S(1)}, bf16[384,128]{1,0:T(8,128)(2,1)S(1)}, u32[]{:S(2)}, u32[]{:S(2)}) collective-permute-start(bf16[384,128]{1,0:T(8,128)(2,1)S(1)} %get-tuple-element.773), channel_id=1, source_target_pairs={{0,4},{4,8},{8,12},{12,16},{16,20},{20,24},{24,28},{1,5},{5,9},{9,... | collective-permute-start | bytes 294920 | tf_op jit(solution)/shard_map/while/body/eval_jaxpr/ppermute | solution.py:15
  125.3 0.7 fusion.95
  125.9 0.7 fusion.94
  126.6 2.0 select_select_fusion.4
  128.6 2.0 iota_add_fusion.6
  131.3 0.9 fusion.96
  132.2 0.6 fusion.99
  132.8 0.7 fusion.98
  134.6 1.4 collective-permute-start.1
  136.0 4.0 %collective-permute-start = (bf16[384,128]{1,0:T(8,128)(2,1)S(1)}, bf16[384,128]{1,0:T(8,128)(2,1)S(1)}, u32[]{:S(2)}, u32[]{:S(2)}) collective-permute-start(bf16[384,128]{1,0:T(8,128)(2,1)S(1)} %get-tuple-element.773), channel_id=1, source_target_pairs={{0,4},{4,8},{8,12},{12,16},{16,20},{20,24},{24,28},{1,5},{5,9},{9,... | collective-permute-start | bytes 294920 | tf_op jit(solution)/shard_map/while/body/eval_jaxpr/ppermute | solution.py:15
  140.2 0.7 fusion.95
  140.9 0.7 fusion.94
  141.6 2.0 select_select_fusion.4
  143.5 2.0 iota_add_fusion.6
  146.2 0.9 fusion.96
  147.2 0.6 fusion.99
  147.7 0.7 fusion.98
  149.5 1.4 collective-permute-start.1
  151.0 4.9 %collective-permute-start = (bf16[384,128]{1,0:T(8,128)(2,1)S(1)}, bf16[384,128]{1,0:T(8,128)(2,1)S(1)}, u32[]{:S(2)}, u32[]{:S(2)}) collective-permute-start(bf16[384,128]{1,0:T(8,128)(2,1)S(1)} %get-tuple-element.773), channel_id=1, source_target_pairs={{0,4},{4,8},{8,12},{12,16},{16,20},{20,24},{24,28},{1,5},{5,9},{9,... | collective-permute-start | bytes 294920 | tf_op jit(solution)/shard_map/while/body/eval_jaxpr/ppermute | solution.py:15
  156.2 0.7 fusion.95
  156.8 0.7 fusion.94
  157.5 2.0 select_select_fusion.4
  159.5 2.0 iota_add_fusion.6
  162.2 0.9 fusion.96
  163.1 0.6 fusion.99
  163.7 0.7 fusion.98
  165.5 1.0 collective-permute-start.5
  166.5 2.0 collective-permute-start.4
  168.5 7.5 %collective-permute-done.5 = bf16[384,128]{1,0:T(8,128)(2,1)S(1)} collective-permute-done((bf16[384,128]{1,0:T(8,128)(2,1)S(1)}, bf16[384,128]{1,0:T(8,128)(2,1)S(1)}, u32[]{:S(2)}, u32[]{:S(2)}) %collective-permute-start.5) | collective-permute-done | bytes 98336 | tf_op jit(solution)/shard_map/ppermute | solution.py:21
  176.1 1.0 collective-permute-done.4
  177.1 1.1 multiply_convert_fusion
  178.2 0.6 dynamic-slice.27
  179.5 1.3 copy.79
  180.7 40.8 %all-reduce.5.cloned.1.call-done = (bf16[384,2,128]{2,1,0:T(2,128)(2,1)}, bf16[384,2,128]{2,1,0:T(2,128)(2,1)}) async-done(((bf16[384,2,128]{2,1,0:T(2,128)(2,1)}, bf16[384,2,128]{2,1,0:T(2,128)(2,1)}), (bf16[384,2,128]{2,1,0:T(2,128)(2,1)}, bf16[384,2,128]{2,1,0:T(2,128)(2,1)})) %all-reduce.5.cloned.1.call-update) | async-done | bytes 393232
  221.5 1.5 constant_dynamic-slice_fusion.1
  222.9 1.5 constant_dynamic-slice_fusion
  (86 shorter events, 9.1 us)
Async XLA Ops:
  7.2 3.6 %copy-start = (bf16[384,4,128]{2,1,0:T(4,128)(2,1)S(1)}, bf16[384,4,128]{2,1,0:T(4,128)(2,1)}, u32[]{:S(2)}) copy-start(bf16[384,4,128]{2,1,0:T(4,128)(2,1)} %param.20) | copy-start | bytes 1179652
  7.2 3.6 %copy-start.9 = (s32[24]{0:T(128)S(1)}, s32[24]{0:T(128)}, u32[]{:S(2)}) copy-start(s32[24]{0:T(128)} %param.27) | copy-start | bytes 292
  7.2 75.6 %all-gather.2.cloned.1.call-start = ((), (), s32[]{:S(2)}) async-start(), calls=%async_computation | async-start | bytes 7864320 | tf_op jit(solution)/shard_map/all_gather | solution.py:76
  7.9 213.6 %all-reduce.5.cloned.1.call-start = ((), (), s32[]{:S(2)}) async-start(), calls=%async_computation.1 | async-start | bytes 786432
  91.4 0.7 copy-start.1
  98.1 2.5 %copy-start.2 = (bf16[384,512]{1,0:T(8,128)(2,1)S(1)}, bf16[384,512]{1,0:T(8,128)(2,1)}, u32[]{:S(2)}) copy-start(bf16[384,512]{1,0:T(8,128)(2,1)} %copy-done.1) | copy-start | bytes 1179652
  98.1 2.5 %copy-start.5 = (pred[384,384]{0,1:T(8,128)(4,1)S(1)}, pred[384,384]{0,1:T(8,128)(4,1)}, u32[]{:S(2)}) copy-start(pred[384,384]{0,1:T(8,128)(4,1)} %compare_and_fusion.2) | copy-start | bytes 442372
  102.2 1.2 copy-start.3
  102.2 1.2 copy-start.4
  102.2 1.2 copy-start.6
  102.2 1.2 copy-start.7
  102.2 1.2 copy-start.8
  103.6 12.7 %collective-permute-start.1 = (bf16[384,128]{1,0:T(8,128)(2,1)S(1)}, bf16[384,128]{1,0:T(8,128)(2,1)S(1)}, u32[]{:S(2)}, u32[]{:S(2)}) collective-permute-start(bf16[384,128]{1,0:T(8,128)(2,1)S(1)} %get-tuple-element.774), channel_id=1, source_target_pairs={{0,4},{4,8},{8,12},{12,16},{16,20},{20,24},{24,28},{1,5},{5,9},{9,... | collective-permute-start | bytes 294920 | tf_op jit(solution)/shard_map/while/body/eval_jaxpr/ppermute | solution.py:15
  105.4 10.9 %collective-permute-start = (bf16[384,128]{1,0:T(8,128)(2,1)S(1)}, bf16[384,128]{1,0:T(8,128)(2,1)S(1)}, u32[]{:S(2)}, u32[]{:S(2)}) collective-permute-start(bf16[384,128]{1,0:T(8,128)(2,1)S(1)} %get-tuple-element.773), channel_id=1, source_target_pairs={{0,4},{4,8},{8,12},{12,16},{16,20},{20,24},{24,28},{1,5},{5,9},{9,... | collective-permute-start | bytes 294920 | tf_op jit(solution)/shard_map/while/body/eval_jaxpr/ppermute | solution.py:15
  109.1 9.2 %collective-permute-start.3 = (f32[384,128]{1,0:T(8,128)S(1)}, f32[384,128]{1,0:T(8,128)S(1)}, u32[]{:S(2)}, u32[]{:S(2)}) collective-permute-start(f32[384,128]{1,0:T(8,128)S(1)} %get-tuple-element.776), channel_id=1, source_target_pairs={{28,0},{0,4},{4,8},{8,12},{12,16},{16,20},{20,24},{24,28},{29,1},{... | collective-permute-start | bytes 589832 | tf_op jit(solution)/shard_map/while/body/eval_jaxpr/ppermute | solution.py:21
  109.1 9.9 %collective-permute-start.2 = (f32[384,128]{1,0:T(8,128)S(1)}, f32[384,128]{1,0:T(8,128)S(1)}, u32[]{:S(2)}, u32[]{:S(2)}) collective-permute-start(f32[384,128]{1,0:T(8,128)S(1)} %get-tuple-element.775), channel_id=1, source_target_pairs={{28,0},{0,4},{4,8},{8,12},{12,16},{16,20},{20,24},{24,28},{29,1},{... | collective-permute-start | bytes 589832 | tf_op jit(solution)/shard_map/while/body/eval_jaxpr/ppermute | solution.py:21
  119.6 11.2 %collective-permute-start.1 = (bf16[384,128]{1,0:T(8,128)(2,1)S(1)}, bf16[384,128]{1,0:T(8,128)(2,1)S(1)}, u32[]{:S(2)}, u32[]{:S(2)}) collective-permute-start(bf16[384,128]{1,0:T(8,128)(2,1)S(1)} %get-tuple-element.774), channel_id=1, source_target_pairs={{0,4},{4,8},{8,12},{12,16},{16,20},{20,24},{24,28},{1,5},{5,9},{9,... | collective-permute-start | bytes 294920 | tf_op jit(solution)/shard_map/while/body/eval_jaxpr/ppermute | solution.py:15
  121.6 9.2 %collective-permute-start = (bf16[384,128]{1,0:T(8,128)(2,1)S(1)}, bf16[384,128]{1,0:T(8,128)(2,1)S(1)}, u32[]{:S(2)}, u32[]{:S(2)}) collective-permute-start(bf16[384,128]{1,0:T(8,128)(2,1)S(1)} %get-tuple-element.773), channel_id=1, source_target_pairs={{0,4},{4,8},{8,12},{12,16},{16,20},{20,24},{24,28},{1,5},{5,9},{9,... | collective-permute-start | bytes 294920 | tf_op jit(solution)/shard_map/while/body/eval_jaxpr/ppermute | solution.py:15
  125.0 7.8 %collective-permute-start.3 = (f32[384,128]{1,0:T(8,128)S(1)}, f32[384,128]{1,0:T(8,128)S(1)}, u32[]{:S(2)}, u32[]{:S(2)}) collective-permute-start(f32[384,128]{1,0:T(8,128)S(1)} %get-tuple-element.776), channel_id=1, source_target_pairs={{28,0},{0,4},{4,8},{8,12},{12,16},{16,20},{20,24},{24,28},{29,1},{... | collective-permute-start | bytes 589832 | tf_op jit(solution)/shard_map/while/body/eval_jaxpr/ppermute | solution.py:21
  125.1 8.9 %collective-permute-start.2 = (f32[384,128]{1,0:T(8,128)S(1)}, f32[384,128]{1,0:T(8,128)S(1)}, u32[]{:S(2)}, u32[]{:S(2)}) collective-permute-start(f32[384,128]{1,0:T(8,128)S(1)} %get-tuple-element.775), channel_id=1, source_target_pairs={{28,0},{0,4},{4,8},{8,12},{12,16},{16,20},{20,24},{24,28},{29,1},{... | collective-permute-start | bytes 589832 | tf_op jit(solution)/shard_map/while/body/eval_jaxpr/ppermute | solution.py:21
  134.6 11.1 %collective-permute-start.1 = (bf16[384,128]{1,0:T(8,128)(2,1)S(1)}, bf16[384,128]{1,0:T(8,128)(2,1)S(1)}, u32[]{:S(2)}, u32[]{:S(2)}) collective-permute-start(bf16[384,128]{1,0:T(8,128)(2,1)S(1)} %get-tuple-element.774), channel_id=1, source_target_pairs={{0,4},{4,8},{8,12},{12,16},{16,20},{20,24},{24,28},{1,5},{5,9},{9,... | collective-permute-start | bytes 294920 | tf_op jit(solution)/shard_map/while/body/eval_jaxpr/ppermute | solution.py:15
  136.0 9.7 %collective-permute-start = (bf16[384,128]{1,0:T(8,128)(2,1)S(1)}, bf16[384,128]{1,0:T(8,128)(2,1)S(1)}, u32[]{:S(2)}, u32[]{:S(2)}) collective-permute-start(bf16[384,128]{1,0:T(8,128)(2,1)S(1)} %get-tuple-element.773), channel_id=1, source_target_pairs={{0,4},{4,8},{8,12},{12,16},{16,20},{20,24},{24,28},{1,5},{5,9},{9,... | collective-permute-start | bytes 294920 | tf_op jit(solution)/shard_map/while/body/eval_jaxpr/ppermute | solution.py:15
  140.0 7.8 %collective-permute-start.3 = (f32[384,128]{1,0:T(8,128)S(1)}, f32[384,128]{1,0:T(8,128)S(1)}, u32[]{:S(2)}, u32[]{:S(2)}) collective-permute-start(f32[384,128]{1,0:T(8,128)S(1)} %get-tuple-element.776), channel_id=1, source_target_pairs={{28,0},{0,4},{4,8},{8,12},{12,16},{16,20},{20,24},{24,28},{29,1},{... | collective-permute-start | bytes 589832 | tf_op jit(solution)/shard_map/while/body/eval_jaxpr/ppermute | solution.py:21
  140.1 8.9 %collective-permute-start.2 = (f32[384,128]{1,0:T(8,128)S(1)}, f32[384,128]{1,0:T(8,128)S(1)}, u32[]{:S(2)}, u32[]{:S(2)}) collective-permute-start(f32[384,128]{1,0:T(8,128)S(1)} %get-tuple-element.775), channel_id=1, source_target_pairs={{28,0},{0,4},{4,8},{8,12},{12,16},{16,20},{20,24},{24,28},{29,1},{... | collective-permute-start | bytes 589832 | tf_op jit(solution)/shard_map/while/body/eval_jaxpr/ppermute | solution.py:21
  149.5 12.1 %collective-permute-start.1 = (bf16[384,128]{1,0:T(8,128)(2,1)S(1)}, bf16[384,128]{1,0:T(8,128)(2,1)S(1)}, u32[]{:S(2)}, u32[]{:S(2)}) collective-permute-start(bf16[384,128]{1,0:T(8,128)(2,1)S(1)} %get-tuple-element.774), channel_id=1, source_target_pairs={{0,4},{4,8},{8,12},{12,16},{16,20},{20,24},{24,28},{1,5},{5,9},{9,... | collective-permute-start | bytes 294920 | tf_op jit(solution)/shard_map/while/body/eval_jaxpr/ppermute | solution.py:15
  151.0 10.7 %collective-permute-start = (bf16[384,128]{1,0:T(8,128)(2,1)S(1)}, bf16[384,128]{1,0:T(8,128)(2,1)S(1)}, u32[]{:S(2)}, u32[]{:S(2)}) collective-permute-start(bf16[384,128]{1,0:T(8,128)(2,1)S(1)} %get-tuple-element.773), channel_id=1, source_target_pairs={{0,4},{4,8},{8,12},{12,16},{16,20},{20,24},{24,28},{1,5},{5,9},{9,... | collective-permute-start | bytes 294920 | tf_op jit(solution)/shard_map/while/body/eval_jaxpr/ppermute | solution.py:15
  155.9 7.8 %collective-permute-start.3 = (f32[384,128]{1,0:T(8,128)S(1)}, f32[384,128]{1,0:T(8,128)S(1)}, u32[]{:S(2)}, u32[]{:S(2)}) collective-permute-start(f32[384,128]{1,0:T(8,128)S(1)} %get-tuple-element.776), channel_id=1, source_target_pairs={{28,0},{0,4},{4,8},{8,12},{12,16},{16,20},{20,24},{24,28},{29,1},{... | collective-permute-start | bytes 589832 | tf_op jit(solution)/shard_map/while/body/eval_jaxpr/ppermute | solution.py:21
  156.0 8.9 %collective-permute-start.2 = (f32[384,128]{1,0:T(8,128)S(1)}, f32[384,128]{1,0:T(8,128)S(1)}, u32[]{:S(2)}, u32[]{:S(2)}) collective-permute-start(f32[384,128]{1,0:T(8,128)S(1)} %get-tuple-element.775), channel_id=1, source_target_pairs={{28,0},{0,4},{4,8},{8,12},{12,16},{16,20},{20,24},{24,28},{29,1},{... | collective-permute-start | bytes 589832 | tf_op jit(solution)/shard_map/while/body/eval_jaxpr/ppermute | solution.py:21
  165.5 12.8 %copy-start.10 = (u32[32]{0:T(128)S(1)}, u32[32]{0:T(128)}, u32[]{:S(2)}) copy-start(u32[32]{0:T(128)} %constant.369) | copy-start | bytes 388
  165.5 10.5 %collective-permute-start.5 = (bf16[384,128]{1,0:T(8,128)(2,1)S(1)}, bf16[384,128]{1,0:T(8,128)(2,1)S(1)}, u32[]{:S(2)}, u32[]{:S(2)}) collective-permute-start(bf16[384,128]{1,0:T(8,128)(2,1)S(1)} %convert_element_type.83), channel_id=1, source_target_pairs={{16,0},{20,4},{24,8},{28,12},{0,16},{4,20},{8,24},{12,28},{17,1},{... | collective-permute-start | bytes 294920 | tf_op jit(solution)/shard_map/ppermute | solution.py:21
  166.5 10.6 %collective-permute-start.4 = (bf16[384,128]{1,0:T(8,128)(2,1)S(1)}, bf16[384,128]{1,0:T(8,128)(2,1)S(1)}, u32[]{:S(2)}, u32[]{:S(2)}) collective-permute-start(bf16[384,128]{1,0:T(8,128)(2,1)S(1)} %convert_element_type.79), channel_id=1, source_target_pairs={{16,0},{20,4},{24,8},{28,12},{0,16},{4,20},{8,24},{12,28},{17,1},{... | collective-permute-start | bytes 294920 | tf_op jit(solution)/shard_map/ppermute | solution.py:21
Sparse Core Ops, SparseCore 0:
  9.9 72.8 all-gather.1
  178.4 43.0 all-reduce.4
where the time goes:
time: 232 us; the launch traced here: 231 us
  waiting for transfers between devices  120 us (52%)
  starting transfers between devices  27.8 us (12%)
  matrix products  26.8 us (12%)
  other arithmetic  22.7 us (10%)
  local copies, waits for them, and re-layouts  18.7 us (8%)
  between operations  14.9 us (6%)
    all_gather x1, waiting for transfers between devices, per_device(): lax.all_gather(grad_output, 'tp', axis=0, tiled=True)  68 us
    unnamed x3, waiting for transfers between devices  41.4 us
    ppermute x8, starting transfers between devices, passed_along(): return lax.ppermute(shard, axis, pairs)  22.6 us
    ppermute x10, waiting for transfers between devices, from_behind(): return lax.ppermute(block, axis, route)  10.2 us
    select_n x5, other arithmetic, doc_labels(): return jnp.repeat(labels, block_size, total_repeat_length=row_count)  9.71 us
    dot_general x1, matrix products, per_device(): lax.dot_general(lax.all_gather(grad_output, 'tp', axis=0, tiled=True), ou...  8.64 us
    add x4, other arithmetic, pair_terms(): key_pos = key_rank * row_count + offsets  7.99 us
    gather x9, local copies, waits for them, and re-layouts, doc_labels(): return jnp.repeat(labels, block_size, total_repeat_length=row_count)  5.98 us
  transfers between devices with their start and end apart: 20, of which 7 were waited for; matrix products, arithmetic and copies ran while one was open for 18% of the time, Pallas kernels for 0%

commit v1 on v0

v1 whole, which is shorter than its diff:
```python
import functools
from typing import NamedTuple

import jax
import jax.numpy as jnp
from jax import lax
from jax.experimental import pallas as pl
from jax.experimental.pallas import tpu as pltpu
from jax.sharding import PartitionSpec as P

DOCBLK = 128
RANKS_BACK = 4
TERMS = 3
LABELS = 16
FAR = 32768.0
COST = 1000
LOG2E = 1.4426950408889634
VMEM_LIMIT = 16 * 1024 * 1024


def dot_nt(a, b):
    return lax.dot_general(a, b, (((1,), (1,)), ((), ())), preferred_element_type=jnp.float32)


def dot_nn(a, b):
    return lax.dot_general(a, b, (((1,), (0,)), ((), ())), preferred_element_type=jnp.float32)


def split_terms(columns):
    rows = columns[0].shape[0]
    lane = lax.broadcasted_iota(jnp.int32, (rows, 128), 1)
    packed = jnp.zeros((rows, 128), jnp.float32)
    for h, rest in enumerate(columns):
        for i in range(TERMS):
            term = rest.astype(jnp.bfloat16).astype(jnp.float32)
            packed = jnp.where(lane == TERMS * h + i, term, packed)
            rest = rest - term
    return packed


def head_operand(full, head, heads):
    features = full[:, head * 128 : (head + 1) * 128]
    extra = full[:, heads * 128 :]
    lane = lax.broadcasted_iota(jnp.int32, extra.shape, 1)
    mine = ((lane >= TERMS * head) & (lane < TERMS * (head + 1))) | (lane >= TERMS * heads)
    return jnp.concatenate([features, jnp.where(mine, extra, jnp.zeros_like(extra))], axis=1)


def stack_heads(full, heads):
    return jnp.concatenate([head_operand(full, h, heads) for h in range(heads)], axis=0)


def row_places(peer, segments, chunk, shape, axis, copies):
    index = lax.broadcasted_iota(jnp.int32, shape, axis)
    place, start = index, 0
    for _ in range(copies):
        for j, low, size in segments:
            base = (peer ^ j) * chunk + low
            inside = (index >= start) & (index < start + size)
            place = jnp.where(inside, index - start + base, place)
            start += size
    return place


def prepare_kernel(
    plan, docs, query, attn, lse, key, value, query_out, attn_out, key_out, packed
):
    heads, kv_heads, chunk, scale = plan.heads, plan.kv_heads, plan.chunk, plan.scale
    tokens, width = query.shape
    rank, peer = lax.axis_index("ctx"), lax.axis_index("tp")
    blocks = tokens // DOCBLK
    pad = -heads % 8
    level = lse[...] * (1.0 / scale)
    if pad:
        level = jnp.concatenate([level, jnp.zeros((pad, tokens), jnp.float32)], axis=0)
    level = level.T
    terms = split_terms([level[:, h : h + 1] for h in range(heads)])
    lane = lax.broadcasted_iota(jnp.int32, (DOCBLK, 128), 1)
    labelled = (lane >= TERMS * heads) & (lane < TERMS * heads + LABELS)
    packed[:, :width] = query[...]
    for b in range(blocks):
        rows = slice(b * DOCBLK, (b + 1) * DOCBLK)
        label = TERMS * heads + lax.rem(docs[rank * blocks + b], LABELS)
        packed[rows, width:] = jnp.where(lane == label, 1.0, terms[rows]).astype(jnp.bfloat16)
        unlike = jnp.where(labelled & (lane != label), -FAR, 0.0)
        key_out[rows, 256:] = jnp.where(lane < TERMS * heads, -1.0, unlike).astype(jnp.bfloat16)
    group = peer // plan.sharing
    mine = pl.ds(pl.multiple_of(group * 128, 128), 128)
    key_out[:, :128] = key[:, mine]
    key_out[:, 128:256] = value[:, mine]
    start = 0
    for phase in plan.phases:
        for j, low, size in phase:
            rows = pl.ds(pl.multiple_of((peer ^ j) * chunk + low, 16), size)
            query_out[start : start + size, :] = packed[rows, :]
            attn_out[start : start + size, :] = attn[rows, :]
            start += size


def prepare(plan, docs, query, attn, lse, key, value):
    tokens, width = query.shape
    vmem = pl.BlockSpec(memory_space=pltpu.VMEM)
    return pl.pallas_call(
        functools.partial(prepare_kernel, plan),
        in_specs=[pl.BlockSpec(memory_space=pltpu.SMEM)] + [vmem] * 5,
        out_specs=[vmem] * 3,
        out_shape=[
            jax.ShapeDtypeStruct((tokens, width + 128), jnp.bfloat16),
            jax.ShapeDtypeStruct((tokens, width), jnp.bfloat16),
            jax.ShapeDtypeStruct((tokens, 384), jnp.bfloat16),
        ],
        scratch_shapes=[pltpu.VMEM((tokens, width + 128), jnp.bfloat16)],
        compiler_params=pltpu.CompilerParams(vmem_limit_bytes=VMEM_LIMIT),
        cost_estimate=pl.CostEstimate(flops=COST, bytes_accessed=0, transcendentals=0),
        name="prepare",
    )(docs, query, attn, lse, key, value)


def project_kernel(heads, parts, *refs):
    grads, weight, attn, out = refs[:parts], refs[parts], refs[parts + 1], refs[-1]
    width = weight.shape[0]
    rows = jnp.concatenate([g[...] for g in grads], axis=0) if parts > 1 else grads[0][...]
    deltas = []
    span = 2 * 128 if heads % 2 == 0 else 128
    for low in range(0, width, span):
        part = dot_nt(weight[low : low + span, :], rows).T.astype(jnp.bfloat16)
        out[:, low : low + span] = part
        product = part.astype(jnp.float32) * attn[:, low : low + span].astype(jnp.float32)
        for h in range(span // 128):
            deltas.append(jnp.sum(product[:, h * 128 : (h + 1) * 128], axis=1, keepdims=True))
    out[:, width:] = split_terms(deltas).astype(jnp.bfloat16)


def project(grads, weight, attn, heads):
    rows = sum(g.shape[0] for g in grads)
    width, depth = weight.shape
    vmem = pl.BlockSpec(memory_space=pltpu.VMEM)
    return pl.pallas_call(
        functools.partial(project_kernel, heads, len(grads)),
        in_specs=[vmem] * (len(grads) + 2),
        out_specs=vmem,
        out_shape=jax.ShapeDtypeStruct((rows, width + 128), jnp.bfloat16),
        compiler_params=pltpu.CompilerParams(vmem_limit_bytes=VMEM_LIMIT),
        cost_estimate=pl.CostEstimate(
            flops=COST, bytes_accessed=0, transcendentals=0
        ),
        name="project",
    )(*grads, weight, attn)


def reached(docs, rank, first_row, step, fits, blocks, back):
    if back:
        key_rank, query_rank = rank - step, rank
    else:
        key_rank, query_rank = rank, rank + step
    last = docs.shape[0] - 1
    key_doc = docs[jnp.clip(key_rank * blocks + blocks - 1, 0, last)]
    query_doc = docs[jnp.clip(query_rank * blocks + first_row // DOCBLK, 0, last)]
    return fits & (key_doc >= query_doc)


def first_row_of(plan, phase, peer):
    return functools.reduce(jnp.minimum, [(peer ^ j) * plan.chunk + low for j, low, _ in phase])


def put_rows(plan, peer, out, segments, source):
    at = 0
    for j, low, size in segments:
        place = pl.ds(pl.multiple_of((peer ^ j) * plan.chunk + low, 16), size)
        out[place, :] = source(at, size)
        at += size


def fetch(needed, pairs, sem):
    def copies(s):
        return [
            pltpu.make_async_copy(x, y, sem.at[len(pairs[s]) * s + i])
            for i, (x, y) in enumerate(pairs[s])
        ]

    for s, need in enumerate(needed):

        @pl.when(need)
        def _(s=s):
            for copy in copies(s):
                copy.start()

    def wait(s):
        for copy in copies(s):
            copy.wait()

    return wait


def behind(docs, rank, first_row, blocks):
    core = lax.rem(rank, 2)
    needed = []
    for s in range(6):
        step = 2 * s if s < 3 else 2 * (s - 3) + 2 * core - 1
        fits = (step >= 0) & (step <= RANKS_BACK) & (rank - step >= 0)
        needed.append(reached(docs, rank, first_row, step, fits, blocks, True))
    return needed


def early_kernel(plan, parts, docs, *refs):
    heads, scale, phase = plan.heads, plan.scale, plan.phases[0]
    keys, qx, oxs = refs[:6], refs[6], refs[7 : 7 + parts]
    query_out, own_out, other_out, turned, block, sem = refs[7 + parts :]
    rows, tokens = query_out.shape[0], keys[0].shape[0]
    rank, peer = lax.axis_index("ctx"), lax.axis_index("tp")
    needed = behind(docs, rank, first_row_of(plan, phase, peer), plan.blocks)
    wait = fetch(needed, [[(keys[s], block.at[s])] for s in range(6)], sem)
    turned[...] = jnp.zeros_like(turned)
    queries = stack_heads(qx[:rows, :], heads)
    grads = stack_heads(jnp.concatenate([x[...] for x in oxs], axis=0), heads)
    for s in range(6):
        out = own_out.at[s] if s < 3 else other_out.at[s - 3]

        @pl.when(needed[s])
        def _(s=s, out=out):
            wait(s)
            key, value, extra = block[s, :, :128], block[s, :, 128:256], block[s, :, 256:]
            scores = dot_nt(jnp.concatenate([key, extra], axis=1), queries)
            if s == 0:
                place = lax.broadcasted_iota(jnp.int32, scores.shape, 0)
                seats = row_places(peer, phase, plan.chunk, (1, heads * rows), 1, heads)
                scores = jnp.where(place <= seats, scores, -FAR)
            probs = jnp.exp2(scores * (scale * LOG2E))
            dprobs = dot_nt(jnp.concatenate([value, extra], axis=1), grads)
            dscores = (probs * dprobs).astype(jnp.bfloat16)
            turned[...] += dot_nn(key.T, dscores)
            out[:, :128] = (dot_nn(dscores, queries[:, :128]) * scale).astype(out.dtype)
            out[:, 128:] = dot_nn(probs.astype(jnp.bfloat16), grads[:, :128]).astype(out.dtype)

        @pl.when(jnp.logical_not(needed[s]))
        def _(out=out):
            out[...] = jnp.zeros(out.shape, out.dtype)

    for h in range(heads):
        query_out[:, h * 128 : (h + 1) * 128] = (
            (turned[:, h * rows : (h + 1) * rows] * scale).T.astype(jnp.bfloat16)
        )


def early_gradients(plan, docs, keys, qx, oxs):
    rows, tokens = sum(x.shape[0] for x in oxs), keys[0].shape[0]
    vmem, any_place = pl.BlockSpec(memory_space=pltpu.VMEM), pl.BlockSpec(memory_space=pl.ANY)
    return pl.pallas_call(
        functools.partial(early_kernel, plan, len(oxs)),
        in_specs=[pl.BlockSpec(memory_space=pltpu.SMEM)] + [any_place] * 6 + [vmem] * (1 + len(oxs)),
        out_specs=[vmem] * 3,
        out_shape=[
            jax.ShapeDtypeStruct((rows, plan.heads * 128), jnp.bfloat16),
            jax.ShapeDtypeStruct((3, tokens, 256), jnp.bfloat16),
            jax.ShapeDtypeStruct((3, tokens, 256), jnp.bfloat16),
        ],
        scratch_shapes=[
            pltpu.VMEM((128, plan.heads * rows), jnp.float32),
            pltpu.VMEM((6, *keys[0].shape), jnp.bfloat16),
            pltpu.SemaphoreType.DMA((6,)),
        ],
        compiler_params=pltpu.CompilerParams(vmem_limit_bytes=VMEM_LIMIT),
        cost_estimate=pl.CostEstimate(flops=COST, bytes_accessed=0, transcendentals=0),
        name="early_gradients",
    )(docs, *keys, qx, *oxs)


def query_kernel(plan, number, before, docs, *refs):
    heads, scale, phase = plan.heads, plan.scale, plan.phases[number]
    start = sum(size for p in plan.phases[1:number] for _, _, size in p)
    keys, (qx, ox), done = refs[:6], refs[6:8], refs[8 : 8 + before]
    out, total, block, sem = refs[8 + before :]
    rows = ox.shape[0]
    rank, peer = lax.axis_index("ctx"), lax.axis_index("tp")
    needed = behind(docs, rank, first_row_of(plan, phase, peer), plan.blocks)
    wait = fetch(needed, [[(keys[s], block.at[s])] for s in range(6)], sem)
    total[...] = jnp.zeros_like(total)
    queries = stack_heads(qx[start : start + rows, :], heads)
    grads = stack_heads(ox[...], heads)
    for s in range(6):

        @pl.when(needed[s])
        def _(s=s):
            wait(s)
            key, value, extra = block[s, :, :128], block[s, :, 128:256], block[s, :, 256:]
            scores = dot_nt(queries, jnp.concatenate([key, extra], axis=1))
            if s == 0:
                place = lax.broadcasted_iota(jnp.int32, scores.shape, 1)
                seats = jnp.concatenate(
                    [row_places(peer, phase, plan.chunk, (rows, 1), 0, 1)] * heads, axis=0
                )
                scores = jnp.where(place <= seats, scores, -FAR)
            probs = jnp.exp2(scores * (scale * LOG2E))
            dprobs = dot_nt(grads, jnp.concatenate([value, extra], axis=1))
            total[...] += dot_nn((probs * dprobs).astype(jnp.bfloat16), key)

    def mine(at, size):
        return jnp.concatenate(
            [
                (total[h * rows + at : h * rows + at + size, :] * scale).astype(jnp.bfloat16)
                for h in range(heads)
            ],
            axis=1,
        )

    if before:
        for ref, segments in zip(done, plan.phases[:before], strict=True):
            put_rows(plan, peer, out, segments, lambda at, size, ref=ref: ref[at : at + size, :])
        put_rows(plan, peer, out, phase, mine)
    else:
        out[...] = mine(0, rows)


def query_gradient(plan, number, docs, keys, qx, ox, done):
    rows, width = ox.shape[0], plan.heads * 128
    out_rows = sum(d.shape[0] for d in done) + rows
    vmem, any_place = pl.BlockSpec(memory_space=pltpu.VMEM), pl.BlockSpec(memory_space=pl.ANY)
    return pl.pallas_call(
        functools.partial(query_kernel, plan, number, len(done)),
        in_specs=[pl.BlockSpec(memory_space=pltpu.SMEM)] + [any_place] * 6 + [vmem] * (2 + len(done)),
        out_specs=vmem,
        out_shape=jax.ShapeDtypeStruct((out_rows, width), jnp.bfloat16),
        scratch_shapes=[
            pltpu.VMEM((plan.heads * rows, 128), jnp.float32),
            pltpu.VMEM((6, *keys[0].shape), jnp.bfloat16),
            pltpu.SemaphoreType.DMA((6,)),
        ],
        compiler_params=pltpu.CompilerParams(vmem_limit_bytes=VMEM_LIMIT),
        cost_estimate=pl.CostEstimate(flops=COST, bytes_accessed=0, transcendentals=0),
        name="query_gradient",
    )(docs, *keys, qx, ox, *done)


def key_kernel(plan, number, first, last, docs, own, *refs):
    heads, scale, phase = plan.heads, plan.scale, plan.phases[number]
    start = sum(size for p in plan.phases[1:number] for _, _, size in p)
    qxs, oxs = refs[:6], refs[6:12]
    before = refs[12:-5]
    out, total, queries_in, grads_in, sem = refs[-5:]
    rows = oxs[0].shape[0]
    rank, peer = lax.axis_index("ctx"), lax.axis_index("tp")
    core = lax.rem(rank, 2)
    first_row = first_row_of(plan, phase, peer)
    needed = []
    for s in range(6):
        step = 2 * s if s < 3 else 2 * (s - 3) - 2 * core + 1
        fits = (step >= 0) & (step <= RANKS_BACK) & (rank + step < plan.ranks)
        needed.append(reached(docs, rank, first_row, step, fits, plan.blocks, False))
    wait = fetch(
        needed,
        [
            [
                (qxs[s].at[pl.ds(start, rows)], queries_in.at[s]),
                (oxs[s], grads_in.at[s]),
            ]
            for s in range(6)
        ],
        sem,
    )
    total[...] = sum((x[...].astype(jnp.float32) for x in before), jnp.zeros_like(total))
    for s in range(6):

        @pl.when(needed[s])
        def _(s=s):
            wait(s)
            block = own[...]
            key, value, extra = block[:, :128], block[:, 128:256], block[:, 256:]
            queries = stack_heads(queries_in[s], heads)
            grads = stack_heads(grads_in[s], heads)
            scores = dot_nt(jnp.concatenate([key, extra], axis=1), queries)
            if s == 0:
                place = lax.broadcasted_iota(jnp.int32, scores.shape, 0)
                seats = row_places(peer, phase, plan.chunk, (1, heads * rows), 1, heads)
                scores = jnp.where(place <= seats, scores, -FAR)
            probs = jnp.exp2(scores * (scale * LOG2E))
            dprobs = dot_nt(jnp.concatenate([value, extra], axis=1), grads)
            total[:, :128] += scale * dot_nn(
                (probs * dprobs).astype(jnp.bfloat16), queries[:, :128]
            )
            total[:, 128:] += dot_nn(probs.astype(jnp.bfloat16), grads[:, :128])

    out[...] = total[...].astype(out.dtype)


def key_gradient(plan, number, docs, own, qxs, oxs, before, last):
    tokens, rows = own.shape[0], oxs[0].shape[0]
    vmem, any_place = pl.BlockSpec(memory_space=pltpu.VMEM), pl.BlockSpec(memory_space=pl.ANY)
    return pl.pallas_call(
        functools.partial(key_kernel, plan, number, not before, last),
        in_specs=[pl.BlockSpec(memory_space=pltpu.SMEM), vmem]
        + [any_place] * 12
        + [vmem] * len(before),
        out_specs=vmem,
        out_shape=jax.ShapeDtypeStruct((tokens, 256), jnp.bfloat16 if last else jnp.float32),
        scratch_shapes=[
            pltpu.VMEM((tokens, 256), jnp.float32),
            pltpu.VMEM((6, rows, qxs[0].shape[1]), jnp.bfloat16),
            pltpu.VMEM((6, *oxs[0].shape), jnp.bfloat16),
            pltpu.SemaphoreType.DMA((12,)),
        ],
        compiler_params=pltpu.CompilerParams(vmem_limit_bytes=VMEM_LIMIT),
        cost_estimate=pl.CostEstimate(flops=COST, bytes_accessed=0, transcendentals=0),
        name="key_gradient",
    )(docs, own, *qxs, *oxs, *before)


def shift(x, axis, by):
    peers = lax.axis_size(axis)
    return lax.ppermute(x, axis, [(i, i + by) for i in range(peers) if 0 <= i + by < peers])


def swap(x, axis, bits):
    return lax.ppermute(x, axis, [(i, i ^ bits) for i in range(lax.axis_size(axis))])


def reach_out(x, direction, relay):
    near = shift(x, "ctx", 2 * direction)
    return near, shift(near, "ctx", 2 * direction) if relay else shift(x, "ctx", 4 * direction)


def after(x, others):
    return after_all([x], others)[0]


def after_all(xs, others):
    return list(lax.optimization_barrier((*xs, *others))[: len(xs)])


class Plan(NamedTuple):
    heads: int
    kv_heads: int
    sharing: int
    chunk: int
    blocks: int
    ranks: int
    scale: float
    steps: tuple
    phases: tuple


def transfer_steps(peers, chunk):
    bits = [1 << b for b in range(peers.bit_length() - 1)]
    steps = []
    steps.append([(b, 0, chunk, b) for b in bits])
    for count in range(2, len(bits) + 1):
        size = chunk // count
        cuts = [(0, size)]
        for low, length in cuts:
            steps.append(
                [
                    (j, i * size + low, length, b)
                    for j in range(peers)
                    if j.bit_count() == count
                    for i, b in enumerate([b for b in bits if j & b])
                ]
            )
    return steps


def merged(pieces):
    joined = []
    for j, low, size in sorted(pieces):
        if joined and joined[-1][0] == j and joined[-1][1] + joined[-1][2] == low:
            joined[-1] = (j, joined[-1][1], joined[-1][2] + size)
        else:
            joined.append((j, low, size))
    return tuple(joined)


def rows_held(held, j, low, size):
    found, place = [], low
    while place < low + size:
        for (at, start, length), piece in held.items():
            if at == j and start <= place < start + length:
                stop = min(low + size, start + length)
                found.append(piece if (place, stop) == (start, start + length) else piece[place - start : stop - start])
                place = stop
                break
    return found[0] if len(found) == 1 else jnp.concatenate(found, axis=0)


def per_device(
    queries, key_tensor, value_tensor, attn_output, logsumexp_rows, grad_output, out_proj, block_doc
):
    tokens, heads, features = queries.shape
    kv_heads = key_tensor.shape[1]
    ranks, peers = lax.axis_size("ctx"), lax.axis_size("tp")
    chunk = tokens // peers
    peer = lax.axis_index("tp")
    steps = transfer_steps(peers, chunk)
    arrivals = [[(0, 0, chunk)] + [piece[:3] for piece in steps[0]]]
    arrivals += [[piece[:3] for piece in step] for step in steps[1:]]
    sharing = peers // kv_heads
    plan = Plan(
        heads, kv_heads, sharing, chunk, tokens // DOCBLK, ranks, features**-0.5, (),
        tuple(merged(pieces) for pieces in arrivals),
    )

    qx, attn, keys_own = prepare(
        plan,
        block_doc,
        queries.reshape(tokens, heads * features),
        attn_output.reshape(tokens, heads * features),
        logsumexp_rows,
        key_tensor.reshape(tokens, kv_heads * features),
        value_tensor.reshape(tokens, kv_heads * features),
    )
    held = {(0, 0, chunk): grad_output}

    def transfer(step):
        held.update(
            {
                (j, low, size): swap(rows_held(held, j ^ b, low, size), "tp", b)
                for j, low, size, b in step
            }
        )

    def projected(pieces, at):
        parts = [held[p] for p in sorted(pieces)]
        size = sum(p[2] for p in pieces)
        if any(p.shape[0] % 16 for p in parts):
            parts = [jnp.concatenate(parts, axis=0)]
        return project(parts, out_proj, attn[at : at + size], heads)

    def swapped(xs):
        return [swap(x, "ctx", 1) for x in xs]

    transfer(steps[0])
    first = projected([(0, 0, chunk)], 0)
    keys = [keys_own, *reach_out(keys_own, 1, False)]
    early = sum(p[2] for p in plan.phases[0])
    late = qx[early:]
    lates = [late, *reach_out(late, -1, False)]
    keys += swapped(after_all(keys, [lates[-1]]))
    lates += swapped(after_all(lates, [keys[-1]]))
    pieces = [p[:3] for p in steps[0]]
    for piece, rows in zip(pieces, after_all([held[p] for p in pieces], [lates[-1]]), strict=True):
        held[piece] = rows

    for step in steps[1:]:
        transfer(step)
    second = projected(pieces, chunk)
    query_part, own_part, other_part = early_gradients(plan, block_doc, keys, qx, [first, second])
    summed = own_part.astype(jnp.float32) + swap(other_part, "ctx", 1).astype(jnp.float32)
    hop = shift(summed[2].astype(jnp.bfloat16), "ctx", -2)
    hop = shift((summed[1] + hop.astype(jnp.float32)).astype(jnp.bfloat16), "ctx", -2)
    chained = summed[0] + hop.astype(jnp.float32)

    at = early
    oxs = []
    for pieces in arrivals[1:]:
        ox = projected(pieces, at)
        oxs.append([ox, *reach_out(ox, -1, False)])
        at += sum(p[2] for p in pieces)
    for i in range(len(oxs)):
        oxs[i] += swapped(oxs[i])
    total = None
    numbers = range(1, len(plan.phases))
    for i in numbers:
        last = i == numbers[-1]
        before = ([] if total is None else [total]) + ([chained] if last else [])
        total = key_gradient(plan, i, block_doc, keys_own, lates, oxs[i - 1], before, last)
    query_parts = [query_part]
    for i in numbers:
        done = query_parts if i == numbers[-1] else []
        query_parts.append(
            query_gradient(plan, i, block_doc, keys, late, after(oxs[i - 1][0], [total]), done)
        )
    grad_query = query_parts[-1].reshape(tokens, heads, features)
    group = peer // sharing

    def for_peer(j):
        return lax.dynamic_slice_in_dim(total, (peer ^ j) * chunk, chunk, 0)

    sums = []
    for own in range(kv_heads):
        terms = [
            for_peer(j) if j == 0 else swap(for_peer(j), "tp", j)
            for j in range(own * sharing, (own + 1) * sharing)
        ]
        sums.append(sum(t.astype(jnp.float32) for t in terms).astype(jnp.bfloat16))
    by_head = jnp.stack(
        [
            functools.reduce(
                lambda a, b: jnp.where(group ^ h == b[0], b[1], a), enumerate(sums), sums[0]
            )
            for h in range(kv_heads)
        ],
        axis=1,
    )
    return grad_query, by_head[:, :, :features], by_head[:, :, features:]


def solution(mesh):
    placed = (
        P("ctx", "tp", None),
        P("ctx", None, None),
        P("ctx", None, None),
        P("ctx", "tp", None),
        P("tp", "ctx"),
        P(("ctx", "tp"), None),
        P("tp", None),
        P(),
    )
    return jax.shard_map(
        per_device,
        mesh=mesh,
        in_specs=placed,
        out_specs=(
            P("ctx", "tp", None),
            P(("ctx", "tp"), None, None),
            P(("ctx", "tp"), None, None),
        ),
        check_vma=False,
    )
```

time: 232 us -> 103 us (0.44)
  waiting for transfers between devices: 120 us -> 47.9 us
  matrix products: 26.8 us -> 0 us
  other arithmetic: 22.7 us -> 1.27 us
  Pallas kernels: 0 us -> 14.9 us
  between operations: 14.9 us -> 1.02 us
  local copies, waits for them, and re-layouts: 18.7 us -> 8.08 us
    all_gather x1 -> x0, waiting for transfers between devices: 68 us -> none  [per_device(): lax.all_gather(grad_output, 'tp', axis=0, tiled=True)]
    unnamed x3 -> x0, waiting for transfers between devices: 41.4 us -> none
    ppermute x18 -> x25, waiting for transfers between devices: 10.2 us -> 47.9 us  [the longest x8 38.5 us: shift(): lax.ppermute(x, axis, [(i, i + by) for i in range(peers) if 0 <= i + by <...]
    dot_general x26 -> x0, matrix products: 26.8 us -> none  [the longest x1 8.64 us: per_device(): lax.dot_general(lax.all_gather(grad_output, 'tp', axis=0, tiled=True), ou...]
    pallas_call x0 -> x7, Pallas kernels: none -> 14.9 us  [the longest x3 7.88 us: project(): pl.pallas_call(functools.partial(project_kernel, heads, len(grads)), in_s...]
    select_n x5 -> x0, other arithmetic: 9.71 us -> none  [doc_labels(): return jnp.repeat(labels, block_size, total_repeat_length=row_count)]
    add x8 -> x2, other arithmetic: 8 us -> 1.17 us  [the longest x1 1.04 us: per_device(): chained = summed[0] + hop.astype(jnp.float32)]
    gather x9 -> x0, local copies, waits for them, and re-layouts: 5.98 us -> none  [doc_labels(): return jnp.repeat(labels, block_size, total_repeat_length=row_count)]
  transfers between devices with their start and end apart: 20 -> 25, of which waited for: 7 -> 10; matrix products, arithmetic and copies ran while one was open for 18% -> 4% of each run, Pallas kernels for 0% -> 10%
where the time goes in v1:
time: 103 us; the launch traced here: 102 us
  waiting for transfers between devices  47.9 us (47%)
  starting transfers between devices  28.9 us (28%)
  Pallas kernels  14.9 us (14%)
  local copies, waits for them, and re-layouts  8.08 us (8%)
  other arithmetic  1.27 us (1%)
    ppermute x8, waiting for transfers between devices, shift(): lax.ppermute(x, axis, [(i, i + by) for i in range(peers) if 0 <= i + by <...  38.5 us
    ppermute x8, starting transfers between devices, shift(): lax.ppermute(x, axis, [(i, i + by) for i in range(peers) if 0 <= i + by <...  15.8 us
    ppermute x17, starting transfers between devices, swap(): lax.ppermute(x, axis, [(i, i ^ bits) for i in range(lax.axis_size(axis))])  13.2 us
    ppermute x17, waiting for transfers between devices, swap(): lax.ppermute(x, axis, [(i, i ^ bits) for i in range(lax.axis_size(axis))])  9.42 us
    pallas_call x3, Pallas kernels, project(): pl.pallas_call(functools.partial(project_kernel, heads, len(grads)), in_s...  7.88 us
    unnamed x16, local copies, waits for them, and re-layouts  4.73 us
    pallas_call x1, Pallas kernels, early_gradients(): pl.pallas_call(functools.partial(early_kernel, plan, len(oxs)), in_specs=...  2.84 us
  transfers between devices with their start and end apart: 25, of which 10 were waited for; matrix products, arithmetic and copies ran while one was open for 4% of the time, Pallas kernels for 10%

profile of v1, /device:TPU:0, one launch (start us, length us, event | category | flops | bytes accessed | tf_op | source)
XLA Modules:
  0.0 102.1 jit_solution(6386290612669636227)
XLA Ops:
  0.6 3.0 %collective-permute-start.6 = (bf16[96,8192]{1,0:T(8,128)(2,1)}, bf16[96,8192]{1,0:T(8,128)(2,1)S(1)}, u32[]{:S(2)}, u32[]{:S(2)}) collective-permute-start(bf16[96,8192]{1,0:T(8,128)(2,1)} %refs_0_.1), channel_id=1, source_target_pairs={{0,1},{1,0},{2,3},{3,2},{4,5},{5,4},{6,7},{7,6},{8,9},{9,8},{10,11... | collective-permute-start | bytes 4718600 | tf_op jit(solution)/shard_map/ppermute | solution.py:413
  3.6 1.5 %collective-permute-start.7 = (bf16[96,8192]{1,0:T(8,128)(2,1)}, bf16[96,8192]{1,0:T(8,128)(2,1)S(1)}, u32[]{:S(2)}, u32[]{:S(2)}) collective-permute-start(bf16[96,8192]{1,0:T(8,128)(2,1)} %refs_0_.1), channel_id=1, source_target_pairs={{0,2},{1,3},{2,0},{3,1},{4,6},{5,7},{6,4},{7,5},{8,10},{9,11},{10,... | collective-permute-start | bytes 4718600 | tf_op jit(solution)/shard_map/ppermute | solution.py:413
  5.2 1.1 %copy_bitcast_fusion.2 = (bf16[384,256]{1,0:T(8,128)(2,1)S(1)}, bf16[384,256]{1,0:T(8,128)(2,1)S(1)}) fusion(bf16[48,8,2,128]{3,2,1,0:T(2,128)(2,1)} %bitcast.32, bf16[48,8,2,128]{3,2,1,0:T(2,128)(2,1)} %bitcast.33), kind=kLoop, calls=%fused_computation.10 | loop fusion | bytes 786432 | tf_op jit(solution)/shard_map/reshape | solution.py:506
  6.3 1.2 %copy_bitcast_fusion = (bf16[384,512]{1,0:T(8,128)(2,1)S(1)}, bf16[384,512]{1,0:T(8,128)(2,1)S(1)}) fusion(bf16[48,8,4,128]{3,2,1,0:T(4,128)(2,1)} %bitcast.30, bf16[48,8,4,128]{3,2,1,0:T(4,128)(2,1)} %bitcast.31), kind=kLoop, calls=%fused_computation.1 | loop fusion | bytes 1572864 | tf_op jit(solution)/shard_map/reshape | solution.py:503
  7.5 0.0 copy-start.1
  7.5 1.2 %prepare.1 = (bf16[384,640]{1,0:T(8,128)(2,1)S(1)}, bf16[384,512]{1,0:T(8,128)(2,1)S(1)}, bf16[384,384]{1,0:T(8,128)(2,1)S(1)}) custom-call(s32[24]{0:T(128)S(1)} %copy-done.2, bf16[384,512]{1,0:T(8,128)(2,1)S(1)} %get-tuple-element.46.query, bf16[384,512]{1,0:T(8,128)(2,1)S(1)} %get-tuple-element.45.attn, f32[4,384]{1,0:T(4,128)S(1)} %copy-done.3, ...), custom_call_target="tpu_custom_call" | custom-call | flops 1000 | tf_op jit(solution)/shard_map/prepare/pallas_call | solution.py:103
  8.7 4.5 %collective-permute-start.1 = (bf16[384,384]{1,0:T(8,128)(2,1)S(1)}, bf16[384,384]{1,0:T(8,128)(2,1)S(1)}, u32[]{:S(2)}, u32[]{:S(2)}) collective-permute-start(bf16[384,384]{1,0:T(8,128)(2,1)S(1)} %get-tuple-element.20.refs_0_.own), channel_id=1, source_target_pairs={{0,16},{4,20},{8,24},{12,28},{1,17},{5,21},{9,25},{13,29},{2,18},{... | collective-permute-start | bytes 884744 | tf_op jit(solution)/shard_map/ppermute | solution.py:409
  13.2 3.5 %collective-permute-start = (bf16[384,384]{1,0:T(8,128)(2,1)S(1)}, bf16[384,384]{1,0:T(8,128)(2,1)S(1)}, u32[]{:S(2)}, u32[]{:S(2)}) collective-permute-start(bf16[384,384]{1,0:T(8,128)(2,1)S(1)} %get-tuple-element.20.refs_0_.own), channel_id=1, source_target_pairs={{0,8},{4,12},{8,16},{12,20},{16,24},{20,28},{1,9},{5,13},{9,17},{1... | collective-permute-start | bytes 884744 | tf_op jit(solution)/shard_map/ppermute | solution.py:409
  16.8 1.3 %collective-permute-start.2 = (bf16[96,640]{1,0:T(8,128)(2,1)S(1)}, bf16[96,640]{1,0:T(8,128)(2,1)S(1)}, u32[]{:S(2)}, u32[]{:S(2)}) collective-permute-start(bf16[96,640]{1,0:T(8,128)(2,1)S(1)} %slice.34.refs_0_.refs_6_), channel_id=1, source_target_pairs={{16,0},{20,4},{24,8},{28,12},{17,1},{21,5},{25,9},{29,13},{18,2},{... | collective-permute-start | bytes 368648 | tf_op jit(solution)/shard_map/ppermute | solution.py:409
  18.1 7.8 %collective-permute-done.2.refs_2_ = bf16[96,640]{1,0:T(8,128)(2,1)S(1)} collective-permute-done((bf16[96,640]{1,0:T(8,128)(2,1)S(1)}, bf16[96,640]{1,0:T(8,128)(2,1)S(1)}, u32[]{:S(2)}, u32[]{:S(2)}) %collective-permute-start.2) | collective-permute-done | bytes 122912 | tf_op jit(solution)/shard_map/ppermute | solution.py:409
  25.9 0.0 collective-permute-start.5
  25.9 1.3 %collective-permute-start.8 = (bf16[96,640]{1,0:T(8,128)(2,1)S(1)}, bf16[96,640]{1,0:T(8,128)(2,1)S(1)}, u32[]{:S(2)}, u32[]{:S(2)}) collective-permute-start(bf16[96,640]{1,0:T(8,128)(2,1)S(1)} %slice.34.refs_0_.refs_6_), channel_id=1, source_target_pairs={{8,0},{12,4},{16,8},{20,12},{24,16},{28,20},{9,1},{13,5},{17,9},{2... | collective-permute-start | bytes 368648 | tf_op jit(solution)/shard_map/ppermute | solution.py:409
  27.2 0.6 collective-permute-start.3
  27.7 11.2 %collective-permute-done.8.refs_1_ = bf16[96,640]{1,0:T(8,128)(2,1)S(1)} collective-permute-done((bf16[96,640]{1,0:T(8,128)(2,1)S(1)}, bf16[96,640]{1,0:T(8,128)(2,1)S(1)}, u32[]{:S(2)}, u32[]{:S(2)}) %collective-permute-start.8) | collective-permute-done | bytes 122912 | tf_op jit(solution)/shard_map/ppermute | solution.py:409
  38.9 0.0 collective-permute-start.4
  38.9 0.0 collective-permute-done.5.refs_5_
  39.0 0.5 collective-permute-start.9
  39.5 0.0 copy-start
  39.5 3.4 %copy-done = bf16[512,8192]{1,0:T(8,128)(2,1)S(1)} copy-done((bf16[512,8192]{1,0:T(8,128)(2,1)S(1)}, bf16[512,8192]{1,0:T(8,128)(2,1)}, u32[]{:S(2)}) %copy-start) | copy-done | bytes 8388632
  42.9 2.6 %project.4.refs_7_ = bf16[96,640]{1,0:T(8,128)(2,1)S(1)} custom-call(bf16[96,8192]{1,0:T(8,128)(2,1)S(1)} %copy-done.1, bf16[512,8192]{1,0:T(8,128)(2,1)S(1)} %copy-done, bf16[96,512]{1,0:T(8,128)(2,1)S(1)} %get-tuple-element.36.refs_2_), custom_call_target="tpu_custom_call" | custom-call | flops 1000 | tf_op jit(solution)/shard_map/project/pallas_call | solution.py:138
  45.5 0.0 slice-start
  45.5 0.0 slice-start.1
  45.6 0.0 collective-permute-done.9.refs_5_
  45.6 0.0 collective-permute-done.7.refs_1_
  45.6 2.6 %project.5.refs_8_ = bf16[192,640]{1,0:T(8,128)(2,1)S(1)} custom-call(bf16[96,8192]{1,0:T(8,128)(2,1)S(1)} %collective-permute-done.6.refs_0_, bf16[96,8192]{1,0:T(8,128)(2,1)S(1)} %collective-permute-done.7.refs_1_, bf16[512,8192]{1,0:T(8,128)(2,1)S(1)} %copy-done, bf16[192,512]{1,0:T(8,128)(2,1)S(1)} %slice.39.refs_3_), custom_call_target="tpu_custom_call" | custom-call | flops 1000 | tf_op jit(solution)/shard_map/project/pallas_call | solution.py:138
  48.2 0.0 collective-permute-done.4.refs_4_
  48.2 2.8 %early_gradients.1 = (bf16[288,512]{1,0:T(8,128)(2,1)S(1)}, bf16[3,384,256]{2,1,0:T(8,128)(2,1)S(1)}, bf16[3,384,256]{2,1,0:T(8,128)(2,1)S(1)}) custom-call(s32[24]{0:T(128)S(1)} %copy-done.2, bf16[384,384]{1,0:T(8,128)(2,1)S(1)} %get-tuple-element.20.refs_0_.own, bf16[384,384]{1,0:T(8,128)(2,1)S(1)} %collective-permute-done.refs_1_, ...), custom_call_target="tpu_custom_call" | custom-call | flops 1000 | tf_op jit(solution)/shard_map/early_gradients/pallas_call | solution.py:248
  51.1 1.5 %collective-permute-start.19 = (bf16[3,384,256]{2,1,0:T(8,128)(2,1)S(1)}, bf16[3,384,256]{2,1,0:T(8,128)(2,1)S(1)}, u32[]{:S(2)}, u32[]{:S(2)}) collective-permute-start(bf16[3,384,256]{2,1,0:T(8,128)(2,1)S(1)} %get-tuple-element.30), channel_id=1, source_target_pairs={{0,4},{4,0},{8,12},{12,8},{16,20},{20,16},{24,28},{28,24},{1,5},{5... | collective-permute-start | bytes 1769480 | tf_op jit(solution)/shard_map/ppermute | solution.py:413
  52.5 0.1 slice.35
  52.6 0.1 slice.36
  52.7 0.6 collective-permute-start.11
  53.2 0.5 collective-permute-start.10
  53.8 0.4 collective-permute-done.19
  54.2 0.1 convert_add_fusion
  54.4 1.3 %collective-permute-start.20 = (bf16[384,256]{1,0:T(8,128)(2,1)S(1)}, bf16[384,256]{1,0:T(8,128)(2,1)S(1)}, u32[]{:S(2)}, u32[]{:S(2)}) collective-permute-start(bf16[384,256]{1,0:T(8,128)(2,1)S(1)} %fusion.3), channel_id=1, source_target_pairs={{8,0},{12,4},{16,8},{20,12},{24,16},{28,20},{9,1},{13,5},{17,9},{2... | collective-permute-start | bytes 589832 | tf_op jit(solution)/shard_map/ppermute | solution.py:409
  55.7 8.5 %collective-permute-done.20 = bf16[384,256]{1,0:T(8,128)(2,1)S(1)} collective-permute-done((bf16[384,256]{1,0:T(8,128)(2,1)S(1)}, bf16[384,256]{1,0:T(8,128)(2,1)S(1)}, u32[]{:S(2)}, u32[]{:S(2)}) %collective-permute-start.20) | collective-permute-done | bytes 196640 | tf_op jit(solution)/shard_map/ppermute | solution.py:409
  64.2 1.3 %collective-permute-start.21 = (bf16[384,256]{1,0:T(8,128)(2,1)S(1)}, bf16[384,256]{1,0:T(8,128)(2,1)S(1)}, u32[]{:S(2)}, u32[]{:S(2)}) collective-permute-start(bf16[384,256]{1,0:T(8,128)(2,1)S(1)} %fusion.1), channel_id=1, source_target_pairs={{8,0},{12,4},{16,8},{20,12},{24,16},{28,20},{9,1},{13,5},{17,9},{2... | collective-permute-start | bytes 589832 | tf_op jit(solution)/shard_map/ppermute | solution.py:409
  65.5 6.7 %collective-permute-done.11.refs_1_ = bf16[48,8192]{1,0:T(8,128)(2,1)S(1)} collective-permute-done((bf16[48,8192]{1,0:T(8,128)(2,1)S(1)}, bf16[48,8192]{1,0:T(8,128)(2,1)S(1)}, u32[]{:S(2)}, u32[]{:S(2)}) %collective-permute-start.11) | collective-permute-done | bytes 786464 | tf_op jit(solution)/shard_map/ppermute | solution.py:413
  72.2 0.2 collective-permute-done.10.refs_0_
  72.4 2.6 %project.3.refs_6_.refs_7_ = bf16[96,640]{1,0:T(8,128)(2,1)S(1)} custom-call(bf16[48,8192]{1,0:T(8,128)(2,1)S(1)} %collective-permute-done.10.refs_0_, bf16[48,8192]{1,0:T(8,128)(2,1)S(1)} %collective-permute-done.11.refs_1_, bf16[512,8192]{1,0:T(8,128)(2,1)S(1)} %bitcast.29, bf16[96,512]{1,0:T(8,128)(2,1)S(1)} %get-tuple-element.37.refs_3_), custom_call_target="tpu_custom_call" | custom-call | flops 1000 | tf_op jit(solution)/shard_map/project/pallas_call | solution.py:138
  75.1 1.3 %collective-permute-start.15 = (bf16[96,640]{1,0:T(8,128)(2,1)S(1)}, bf16[96,640]{1,0:T(8,128)(2,1)S(1)}, u32[]{:S(2)}, u32[]{:S(2)}) collective-permute-start(bf16[96,640]{1,0:T(8,128)(2,1)S(1)} %project.3.refs_6_.refs_7_), channel_id=1, source_target_pairs={{16,0},{20,4},{24,8},{28,12},{17,1},{21,5},{25,9},{29,13},{18,2},{... | collective-permute-start | bytes 368648 | tf_op jit(solution)/shard_map/ppermute | solution.py:409
  76.4 1.3 %collective-permute-start.14 = (bf16[96,640]{1,0:T(8,128)(2,1)S(1)}, bf16[96,640]{1,0:T(8,128)(2,1)S(1)}, u32[]{:S(2)}, u32[]{:S(2)}) collective-permute-start(bf16[96,640]{1,0:T(8,128)(2,1)S(1)} %project.3.refs_6_.refs_7_), channel_id=1, source_target_pairs={{8,0},{12,4},{16,8},{20,12},{24,16},{28,20},{9,1},{13,5},{17,9},{2... | collective-permute-start | bytes 368648 | tf_op jit(solution)/shard_map/ppermute | solution.py:409
  77.7 0.1 collective-permute-start.12
  77.8 0.5 collective-permute-start.13
  78.3 11.0 %collective-permute-done.15.refs_8_ = bf16[96,640]{1,0:T(8,128)(2,1)S(1)} collective-permute-done((bf16[96,640]{1,0:T(8,128)(2,1)S(1)}, bf16[96,640]{1,0:T(8,128)(2,1)S(1)}, u32[]{:S(2)}, u32[]{:S(2)}) %collective-permute-start.15) | collective-permute-done | bytes 122912 | tf_op jit(solution)/shard_map/ppermute | solution.py:409
  89.2 0.0 collective-permute-start.16
  89.2 0.0 collective-permute-done.14.refs_7_
  89.2 0.5 collective-permute-start.18
  89.7 0.0 collective-permute-done.21
  89.8 0.1 collective-permute-start.17
  89.8 1.0 %fusion.2.refs_12_ = f32[384,256]{1,0:T(8,128)S(1)} fusion(f32[3,384,256]{2,1,0:T(8,128)} %copy-done.4, bf16[384,256]{1,0:T(8,128)(2,1)S(1)} %collective-permute-done.21), kind=kLoop, calls=%fused_computation.8 | loop fusion | flops 196608 | bytes 983040 | tf_op jit(solution)/shard_map/add | solution.py:547
  90.9 0.0 collective-permute-done.12.refs_3_
  90.9 0.0 collective-permute-done.13.refs_4_
  90.9 0.0 collective-permute-done.18.refs_11_
  90.9 0.2 collective-permute-done.17.refs_10_
  91.1 1.7 %key_gradient.1 = bf16[384,256]{1,0:T(8,128)(2,1)S(1)} custom-call(s32[24]{0:T(128)S(1)} %copy-done.2, bf16[384,384]{1,0:T(8,128)(2,1)S(1)} %get-tuple-element.20.refs_0_.own, bf16[96,640]{1,0:T(8,128)(2,1)S(1)} %slice.34.refs_0_.refs_6_, bf16[96,640]{1,0:T(8,128)(2,1)S(1)} %collective-permute-done.8.refs_1_, ...), custom_call_target="tpu_custom_call" | custom-call | flops 1000 | tf_op jit(solution)/shard_map/key_gradient/pallas_call | solution.py:388
  92.8 0.6 collective-permute-start.24
  93.4 3.3 %collective-permute-start.23 = (bf16[96,256]{1,0:T(8,128)(2,1)S(1)}, bf16[96,256]{1,0:T(8,128)(2,1)S(1)}, u32[]{:S(2)}, u32[]{:S(2)}) collective-permute-start(bf16[96,256]{1,0:T(8,128)(2,1)S(1)} %get-tuple-element.41), channel_id=1, source_target_pairs={{0,3},{1,2},{2,1},{3,0},{4,7},{5,6},{6,5},{7,4},{8,11},{9,10},{10,... | collective-permute-start | bytes 147464 | tf_op jit(solution)/shard_map/ppermute | solution.py:413
  96.7 1.3 %query_gradient.1 = bf16[384,512]{1,0:T(8,128)(2,1)S(1)} custom-call(s32[24]{0:T(128)S(1)} %copy-done.2, bf16[384,384]{1,0:T(8,128)(2,1)S(1)} %get-tuple-element.20.refs_0_.own, bf16[384,384]{1,0:T(8,128)(2,1)S(1)} %collective-permute-done.refs_1_, bf16[384,384]{1,0:T(8,128)(2,1)S(1)} %collective-permute-done.1.refs_2_, ...), custom_call_target="tpu_custom_call" | custom-call | flops 1000 | tf_op jit(solution)/shard_map/query_gradient/pallas_call | solution.py:318
  98.0 0.8 reshape.26
  98.8 0.4 collective-permute-done.23
  99.3 1.5 %collective-permute-done.22 = bf16[96,256]{1,0:T(8,128)(2,1)S(1)} collective-permute-done((bf16[96,256]{1,0:T(8,128)(2,1)S(1)}, bf16[96,256]{1,0:T(8,128)(2,1)S(1)}, u32[]{:S(2)}, u32[]{:S(2)}) %collective-permute-start.22) | collective-permute-done | bytes 49184 | tf_op jit(solution)/shard_map/ppermute | solution.py:413
  100.8 0.7 copy.12
  101.5 0.7 copy.11
  (25 shorter events, 0.2 us)
Async XLA Ops:
  0.6 44.9 %collective-permute-start.6 = (bf16[96,8192]{1,0:T(8,128)(2,1)}, bf16[96,8192]{1,0:T(8,128)(2,1)S(1)}, u32[]{:S(2)}, u32[]{:S(2)}) collective-permute-start(bf16[96,8192]{1,0:T(8,128)(2,1)} %refs_0_.1), channel_id=1, source_target_pairs={{0,1},{1,0},{2,3},{3,2},{4,5},{5,4},{6,7},{7,6},{8,9},{9,8},{10,11... | collective-permute-start | bytes 4718600 | tf_op jit(solution)/shard_map/ppermute | solution.py:413
  3.6 41.9 %collective-permute-start.7 = (bf16[96,8192]{1,0:T(8,128)(2,1)}, bf16[96,8192]{1,0:T(8,128)(2,1)S(1)}, u32[]{:S(2)}, u32[]{:S(2)}) collective-permute-start(bf16[96,8192]{1,0:T(8,128)(2,1)} %refs_0_.1), channel_id=1, source_target_pairs={{0,2},{1,3},{2,0},{3,1},{4,6},{5,7},{6,4},{7,5},{8,10},{9,11},{10,... | collective-permute-start | bytes 4718600 | tf_op jit(solution)/shard_map/ppermute | solution.py:413
  5.2 2.4 %copy-start.2 = (s32[24]{0:T(128)S(1)}, s32[24]{0:T(128)}, u32[]{:S(2)}) copy-start(s32[24]{0:T(128)} %docs.7) | copy-start | bytes 292
  5.2 2.4 %copy-start.3 = (f32[4,384]{1,0:T(4,128)S(1)}, f32[4,384]{1,0:T(4,128)}, u32[]{:S(2)}) copy-start(f32[4,384]{1,0:T(4,128)} %lse.1) | copy-start | bytes 18436
  7.5 32.0 %copy-start.1 = (bf16[96,8192]{1,0:T(8,128)(2,1)S(1)}, bf16[96,8192]{1,0:T(8,128)(2,1)}, u32[]{:S(2)}) copy-start(bf16[96,8192]{1,0:T(8,128)(2,1)} %refs_0_.1) | copy-start | bytes 4718596
  8.7 17.1 %collective-permute-start.1 = (bf16[384,384]{1,0:T(8,128)(2,1)S(1)}, bf16[384,384]{1,0:T(8,128)(2,1)S(1)}, u32[]{:S(2)}, u32[]{:S(2)}) collective-permute-start(bf16[384,384]{1,0:T(8,128)(2,1)S(1)} %get-tuple-element.20.refs_0_.own), channel_id=1, source_target_pairs={{0,16},{4,20},{8,24},{12,28},{1,17},{5,21},{9,25},{13,29},{2,18},{... | collective-permute-start | bytes 884744 | tf_op jit(solution)/shard_map/ppermute | solution.py:409
  13.2 12.6 %collective-permute-start = (bf16[384,384]{1,0:T(8,128)(2,1)S(1)}, bf16[384,384]{1,0:T(8,128)(2,1)S(1)}, u32[]{:S(2)}, u32[]{:S(2)}) collective-permute-start(bf16[384,384]{1,0:T(8,128)(2,1)S(1)} %get-tuple-element.20.refs_0_.own), channel_id=1, source_target_pairs={{0,8},{4,12},{8,16},{12,20},{16,24},{20,28},{1,9},{5,13},{9,17},{1... | collective-permute-start | bytes 884744 | tf_op jit(solution)/shard_map/ppermute | solution.py:409
  16.8 9.1 %collective-permute-start.2 = (bf16[96,640]{1,0:T(8,128)(2,1)S(1)}, bf16[96,640]{1,0:T(8,128)(2,1)S(1)}, u32[]{:S(2)}, u32[]{:S(2)}) collective-permute-start(bf16[96,640]{1,0:T(8,128)(2,1)S(1)} %slice.34.refs_0_.refs_6_), channel_id=1, source_target_pairs={{16,0},{20,4},{24,8},{28,12},{17,1},{21,5},{25,9},{29,13},{18,2},{... | collective-permute-start | bytes 368648 | tf_op jit(solution)/shard_map/ppermute | solution.py:409
  25.9 13.1 %collective-permute-start.5 = (bf16[384,384]{1,0:T(8,128)(2,1)S(1)}, bf16[384,384]{1,0:T(8,128)(2,1)S(1)}, u32[]{:S(2)}, u32[]{:S(2)}) collective-permute-start(bf16[384,384]{1,0:T(8,128)(2,1)S(1)} %collective-permute-done.1.refs_2_), channel_id=1, source_target_pairs={{0,4},{4,0},{8,12},{12,8},{16,20},{20,16},{24,28},{28,24},{1,5},{5... | collective-permute-start | bytes 884744 | tf_op jit(solution)/shard_map/ppermute | solution.py:413
  25.9 13.1 %collective-permute-start.8 = (bf16[96,640]{1,0:T(8,128)(2,1)S(1)}, bf16[96,640]{1,0:T(8,128)(2,1)S(1)}, u32[]{:S(2)}, u32[]{:S(2)}) collective-permute-start(bf16[96,640]{1,0:T(8,128)(2,1)S(1)} %slice.34.refs_0_.refs_6_), channel_id=1, source_target_pairs={{8,0},{12,4},{16,8},{20,12},{24,16},{28,20},{9,1},{13,5},{17,9},{2... | collective-permute-start | bytes 368648 | tf_op jit(solution)/shard_map/ppermute | solution.py:409
  27.2 21.1 %collective-permute-start.3 = (bf16[384,384]{1,0:T(8,128)(2,1)S(1)}, bf16[384,384]{1,0:T(8,128)(2,1)S(1)}, u32[]{:S(2)}, u32[]{:S(2)}) collective-permute-start(bf16[384,384]{1,0:T(8,128)(2,1)S(1)} %get-tuple-element.20.refs_0_.own), channel_id=1, source_target_pairs={{0,4},{4,0},{8,12},{12,8},{16,20},{20,16},{24,28},{28,24},{1,5},{5... | collective-permute-start | bytes 884744 | tf_op jit(solution)/shard_map/ppermute | solution.py:413
  38.9 9.3 %collective-permute-start.4 = (bf16[384,384]{1,0:T(8,128)(2,1)S(1)}, bf16[384,384]{1,0:T(8,128)(2,1)S(1)}, u32[]{:S(2)}, u32[]{:S(2)}) collective-permute-start(bf16[384,384]{1,0:T(8,128)(2,1)S(1)} %collective-permute-done.refs_1_), channel_id=1, source_target_pairs={{0,4},{4,0},{8,12},{12,8},{16,20},{20,16},{24,28},{28,24},{1,5},{5... | collective-permute-start | bytes 884744 | tf_op jit(solution)/shard_map/ppermute | solution.py:413
  39.0 6.6 %collective-permute-start.9 = (bf16[96,640]{1,0:T(8,128)(2,1)S(1)}, bf16[96,640]{1,0:T(8,128)(2,1)S(1)}, u32[]{:S(2)}, u32[]{:S(2)}) collective-permute-start(bf16[96,640]{1,0:T(8,128)(2,1)S(1)} %collective-permute-done.2.refs_2_), channel_id=1, source_target_pairs={{0,4},{4,0},{8,12},{12,8},{16,20},{20,16},{24,28},{28,24},{1,5},{5... | collective-permute-start | bytes 368648 | tf_op jit(solution)/shard_map/ppermute | solution.py:413
  39.5 3.4 %copy-start = (bf16[512,8192]{1,0:T(8,128)(2,1)S(1)}, bf16[512,8192]{1,0:T(8,128)(2,1)}, u32[]{:S(2)}) copy-start(bf16[512,8192]{1,0:T(8,128)(2,1)} %refs_2_.3) | copy-start | bytes 25165828
  45.5 26.9 %slice-start = ((s8[8388608]{0:T(1024)(128)(4,1)}), s8[4194304]{0:T(1024)(128)(4,1)S(1)}, s32[]{:S(2)}) async-start(s8[8388608]{0:T(1024)(128)(4,1)} %bitcast.28), calls=%async_computation | async-start | bytes 8388608
  45.5 26.9 %slice-start.1 = ((s8[8388608]{0:T(1024)(128)(4,1)}), s8[4194304]{0:T(1024)(128)(4,1)S(1)}, s32[]{:S(2)}) async-start(s8[8388608]{0:T(1024)(128)(4,1)} %bitcast.28), calls=%async_computation.1 | async-start | bytes 8388608
  51.1 3.1 %collective-permute-start.19 = (bf16[3,384,256]{2,1,0:T(8,128)(2,1)S(1)}, bf16[3,384,256]{2,1,0:T(8,128)(2,1)S(1)}, u32[]{:S(2)}, u32[]{:S(2)}) collective-permute-start(bf16[3,384,256]{2,1,0:T(8,128)(2,1)S(1)} %get-tuple-element.30), channel_id=1, source_target_pairs={{0,4},{4,0},{8,12},{12,8},{16,20},{20,16},{24,28},{28,24},{1,5},{5... | collective-permute-start | bytes 1769480 | tf_op jit(solution)/shard_map/ppermute | solution.py:413
  52.7 19.5 %collective-permute-start.11 = (bf16[48,8192]{1,0:T(8,128)(2,1)S(1)}, bf16[48,8192]{1,0:T(8,128)(2,1)S(1)}, u32[]{:S(2)}, u32[]{:S(2)}) collective-permute-start(bf16[48,8192]{1,0:T(8,128)(2,1)S(1)} %slice.36), channel_id=1, source_target_pairs={{0,2},{1,3},{2,0},{3,1},{4,6},{5,7},{6,4},{7,5},{8,10},{9,11},{10,... | collective-permute-start | bytes 2359304 | tf_op jit(solution)/shard_map/ppermute | solution.py:413
  53.2 19.2 %collective-permute-start.10 = (bf16[48,8192]{1,0:T(8,128)(2,1)S(1)}, bf16[48,8192]{1,0:T(8,128)(2,1)S(1)}, u32[]{:S(2)}, u32[]{:S(2)}) collective-permute-start(bf16[48,8192]{1,0:T(8,128)(2,1)S(1)} %slice.35), channel_id=1, source_target_pairs={{0,1},{1,0},{2,3},{3,2},{4,5},{5,4},{6,7},{7,6},{8,9},{9,8},{10,11... | collective-permute-start | bytes 2359304 | tf_op jit(solution)/shard_map/ppermute | solution.py:413
  54.3 20.7 %copy-start.4 = (f32[3,384,256]{2,1,0:T(8,128)}, f32[3,384,256]{2,1,0:T(8,128)S(1)}, u32[]{:S(2)}) copy-start(f32[3,384,256]{2,1,0:T(8,128)S(1)} %convert_add_fusion) | copy-start | bytes 3538948
  54.4 9.8 %collective-permute-start.20 = (bf16[384,256]{1,0:T(8,128)(2,1)S(1)}, bf16[384,256]{1,0:T(8,128)(2,1)S(1)}, u32[]{:S(2)}, u32[]{:S(2)}) collective-permute-start(bf16[384,256]{1,0:T(8,128)(2,1)S(1)} %fusion.3), channel_id=1, source_target_pairs={{8,0},{12,4},{16,8},{20,12},{24,16},{28,20},{9,1},{13,5},{17,9},{2... | collective-permute-start | bytes 589832 | tf_op jit(solution)/shard_map/ppermute | solution.py:409
  64.2 25.5 %collective-permute-start.21 = (bf16[384,256]{1,0:T(8,128)(2,1)S(1)}, bf16[384,256]{1,0:T(8,128)(2,1)S(1)}, u32[]{:S(2)}, u32[]{:S(2)}) collective-permute-start(bf16[384,256]{1,0:T(8,128)(2,1)S(1)} %fusion.1), channel_id=1, source_target_pairs={{8,0},{12,4},{16,8},{20,12},{24,16},{28,20},{9,1},{13,5},{17,9},{2... | collective-permute-start | bytes 589832 | tf_op jit(solution)/shard_map/ppermute | solution.py:409
  75.1 14.2 %collective-permute-start.15 = (bf16[96,640]{1,0:T(8,128)(2,1)S(1)}, bf16[96,640]{1,0:T(8,128)(2,1)S(1)}, u32[]{:S(2)}, u32[]{:S(2)}) collective-permute-start(bf16[96,640]{1,0:T(8,128)(2,1)S(1)} %project.3.refs_6_.refs_7_), channel_id=1, source_target_pairs={{16,0},{20,4},{24,8},{28,12},{17,1},{21,5},{25,9},{29,13},{18,2},{... | collective-permute-start | bytes 368648 | tf_op jit(solution)/shard_map/ppermute | solution.py:409
  76.4 12.9 %collective-permute-start.14 = (bf16[96,640]{1,0:T(8,128)(2,1)S(1)}, bf16[96,640]{1,0:T(8,128)(2,1)S(1)}, u32[]{:S(2)}, u32[]{:S(2)}) collective-permute-start(bf16[96,640]{1,0:T(8,128)(2,1)S(1)} %project.3.refs_6_.refs_7_), channel_id=1, source_target_pairs={{8,0},{12,4},{16,8},{20,12},{24,16},{28,20},{9,1},{13,5},{17,9},{2... | collective-permute-start | bytes 368648 | tf_op jit(solution)/shard_map/ppermute | solution.py:409
  77.7 13.2 %collective-permute-start.12 = (bf16[96,640]{1,0:T(8,128)(2,1)S(1)}, bf16[96,640]{1,0:T(8,128)(2,1)S(1)}, u32[]{:S(2)}, u32[]{:S(2)}) collective-permute-start(bf16[96,640]{1,0:T(8,128)(2,1)S(1)} %slice.34.refs_0_.refs_6_), channel_id=1, source_target_pairs={{0,4},{4,0},{8,12},{12,8},{16,20},{20,16},{24,28},{28,24},{1,5},{5... | collective-permute-start | bytes 368648 | tf_op jit(solution)/shard_map/ppermute | solution.py:413
  77.8 13.1 %collective-permute-start.13 = (bf16[96,640]{1,0:T(8,128)(2,1)S(1)}, bf16[96,640]{1,0:T(8,128)(2,1)S(1)}, u32[]{:S(2)}, u32[]{:S(2)}) collective-permute-start(bf16[96,640]{1,0:T(8,128)(2,1)S(1)} %collective-permute-done.8.refs_1_), channel_id=1, source_target_pairs={{0,4},{4,0},{8,12},{12,8},{16,20},{20,16},{24,28},{28,24},{1,5},{5... | collective-permute-start | bytes 368648 | tf_op jit(solution)/shard_map/ppermute | solution.py:413
  89.2 1.7 %collective-permute-start.16 = (bf16[96,640]{1,0:T(8,128)(2,1)S(1)}, bf16[96,640]{1,0:T(8,128)(2,1)S(1)}, u32[]{:S(2)}, u32[]{:S(2)}) collective-permute-start(bf16[96,640]{1,0:T(8,128)(2,1)S(1)} %project.3.refs_6_.refs_7_), channel_id=1, source_target_pairs={{0,4},{4,0},{8,12},{12,8},{16,20},{20,16},{24,28},{28,24},{1,5},{5... | collective-permute-start | bytes 368648 | tf_op jit(solution)/shard_map/ppermute | solution.py:413
  89.2 1.7 %collective-permute-start.18 = (bf16[96,640]{1,0:T(8,128)(2,1)S(1)}, bf16[96,640]{1,0:T(8,128)(2,1)S(1)}, u32[]{:S(2)}, u32[]{:S(2)}) collective-permute-start(bf16[96,640]{1,0:T(8,128)(2,1)S(1)} %collective-permute-done.15.refs_8_), channel_id=1, source_target_pairs={{0,4},{4,0},{8,12},{12,8},{16,20},{20,16},{24,28},{28,24},{1,5},{5... | collective-permute-start | bytes 368648 | tf_op jit(solution)/shard_map/ppermute | solution.py:413
  89.8 1.3 %collective-permute-start.17 = (bf16[96,640]{1,0:T(8,128)(2,1)S(1)}, bf16[96,640]{1,0:T(8,128)(2,1)S(1)}, u32[]{:S(2)}, u32[]{:S(2)}) collective-permute-start(bf16[96,640]{1,0:T(8,128)(2,1)S(1)} %collective-permute-done.14.refs_7_), channel_id=1, source_target_pairs={{0,4},{4,0},{8,12},{12,8},{16,20},{20,16},{24,28},{28,24},{1,5},{5... | collective-permute-start | bytes 368648 | tf_op jit(solution)/shard_map/ppermute | solution.py:413
  92.8 6.0 %collective-permute-start.24 = (bf16[96,256]{1,0:T(8,128)(2,1)S(1)}, bf16[96,256]{1,0:T(8,128)(2,1)S(1)}, u32[]{:S(2)}, u32[]{:S(2)}) collective-permute-start(bf16[96,256]{1,0:T(8,128)(2,1)S(1)} %get-tuple-element.40), channel_id=1, source_target_pairs={{0,1},{1,0},{2,3},{3,2},{4,5},{5,4},{6,7},{7,6},{8,9},{9,8},{10,11... | collective-permute-start | bytes 147464 | tf_op jit(solution)/shard_map/ppermute | solution.py:413
  93.4 5.8 %collective-permute-start.23 = (bf16[96,256]{1,0:T(8,128)(2,1)S(1)}, bf16[96,256]{1,0:T(8,128)(2,1)S(1)}, u32[]{:S(2)}, u32[]{:S(2)}) collective-permute-start(bf16[96,256]{1,0:T(8,128)(2,1)S(1)} %get-tuple-element.41), channel_id=1, source_target_pairs={{0,3},{1,2},{2,1},{3,0},{4,7},{5,6},{6,5},{7,4},{8,11},{9,10},{10,... | collective-permute-start | bytes 147464 | tf_op jit(solution)/shard_map/ppermute | solution.py:413
  96.7 4.1 %collective-permute-start.22 = (bf16[96,256]{1,0:T(8,128)(2,1)S(1)}, bf16[96,256]{1,0:T(8,128)(2,1)S(1)}, u32[]{:S(2)}, u32[]{:S(2)}) collective-permute-start(bf16[96,256]{1,0:T(8,128)(2,1)S(1)} %get-tuple-element.42), channel_id=1, source_target_pairs={{0,2},{1,3},{2,0},{3,1},{4,6},{5,7},{6,4},{7,5},{8,10},{9,11},{10,... | collective-permute-start | bytes 147464 | tf_op jit(solution)/shard_map/ppermute | solution.py:413
